TPU v7x, 1024 devices: a whole 4x8x16 slice. The times are simulated.
1024 devices in a mesh: bal: 4 (over y_hi), fsdp: 256 (over z, x, y_lo, core).
Axes of the slice: x: 4, y: 8 (y_hi: 4, y_lo: 2; y = y_hi * 2 + y_lo), z: 16, core: 2. Of those that a mesh axis runs over, the one named last changes fastest.
Arguments:
- patches: bfloat16 [256, 512, 6144], P('fsdp', 'bal'), may hold values from -6 to 6
- projection: bfloat16 [6144, 192], P('fsdp'), may hold values from -0.078125 to 0.078125
- image_ids: int32 [256, 512], P('fsdp'), may hold values from 0 to 7, never falling along the last dimension, each value on 1 to 256 neighbouring positions
- cotangent: bfloat16 [256, 512, 64], P('fsdp', 'bal'), may hold values from -6 to 6
Outputs:
- head_output: bfloat16 [256, 512, 64], P('fsdp', 'bal')
- patch_grads: bfloat16 [256, 512, 6144], P('fsdp', 'bal')
- projection_grad: float32 [6144, 192], P('fsdp')
Inputs may be any that keep to these rules, and one draw needn't show every extreme that they name: `image_ids`: ids never fall along a sequence; every image of 0 to 7 is present, each with 1 to 256 patches, and one has exactly 256.
All inputs are finite; a program needn't handle non-finite values.
Results may differ from a plain program's by a relative error of at most 0.014.
Values may be sent and summed in bfloat16 or wider, within the bound.
A program may use at most 64 MiB of HBM per device.

v0:
```python
import math

import jax
import jax.numpy as jnp
from jax import lax
from jax.sharding import PartitionSpec as P

EPSILON = 1e-06
CONTRACT_LAST = (((1,), (1,)), ((), ()))
CONTRACT_FIRST = (((0,), (0,)), ((), ()))


def norm_rows(values):
    centred = values - jnp.mean(values, axis=-1, keepdims=True)
    inverse = lax.rsqrt(jnp.mean(centred * centred, axis=-1, keepdims=True) + EPSILON)
    return (centred * inverse, inverse)


def norm_backward(upstream, normal, inverse):
    shifted = upstream - jnp.mean(upstream, axis=-1, keepdims=True)
    return inverse * (shifted - normal * jnp.mean(upstream * normal, axis=-1, keepdims=True))


def per_device(patches, projection, image_ids, cotangent):
    head_width = projection.shape[1] // 3
    factor = 1.0 / math.sqrt(head_width)
    local_rows = patches.shape[1]
    normal_x, inverse_x = norm_rows(patches[0].astype(jnp.float32))
    normed = normal_x.astype(jnp.bfloat16)
    gathered = lax.all_gather(projection, "fsdp", axis=0, tiled=True)
    joined_rows = jnp.dot(normed, gathered, preferred_element_type=jnp.float32)
    normal_q, inverse_q = norm_rows(joined_rows[:, :head_width])
    normal_k, inverse_k = norm_rows(joined_rows[:, head_width : 2 * head_width])
    query_rows = normal_q.astype(jnp.bfloat16)
    key_rows = normal_k.astype(jnp.bfloat16)
    value_rows = joined_rows[:, 2 * head_width :].astype(jnp.bfloat16)
    key_whole, value_whole = (
        lax.all_gather(key_rows[None], "bal", axis=1, tiled=True),
        lax.all_gather(value_rows[None], "bal", axis=1, tiled=True),
    )
    key_whole = key_whole[0]
    value_whole = value_whole[0]
    sequence_ids = image_ids[0]
    offset = lax.axis_index("bal") * local_rows
    own_ids = lax.dynamic_slice_in_dim(sequence_ids, offset, local_rows)
    same_image = own_ids[:, None] == sequence_ids[None, :]
    scores = (
        lax.dot_general(query_rows, key_whole, CONTRACT_LAST, preferred_element_type=jnp.float32)
        * factor
    )
    exponent = jnp.where(same_image, jnp.exp(scores), 0.0)
    denominator = jnp.sum(exponent, axis=-1)
    probs = exponent.astype(jnp.bfloat16)
    attended = (
        jnp.dot(probs, value_whole, preferred_element_type=jnp.float32) / denominator[:, None]
    )
    upstream_f = cotangent[0].astype(jnp.float32)
    scaled_grad = (upstream_f / denominator[:, None]).astype(jnp.bfloat16)
    correction = jnp.sum(upstream_f * attended, axis=-1) / denominator
    prob_grad = lax.dot_general(
        scaled_grad, value_whole, CONTRACT_LAST, preferred_element_type=jnp.float32
    )
    score_grad = (probs.astype(jnp.float32) * (prob_grad - correction[:, None])).astype(
        jnp.bfloat16
    )
    query_grad = jnp.dot(score_grad, key_whole, preferred_element_type=jnp.float32) * factor
    key_part = (
        lax.dot_general(score_grad, query_rows, CONTRACT_FIRST, preferred_element_type=jnp.float32)
        * factor
    )
    value_part = lax.dot_general(
        probs, scaled_grad, CONTRACT_FIRST, preferred_element_type=jnp.float32
    )
    key_grad, value_grad = (
        lax.psum_scatter(
            key_part[None].astype(jnp.bfloat16), "bal", scatter_dimension=1, tiled=True
        ).astype(jnp.float32),
        lax.psum_scatter(
            value_part[None].astype(jnp.bfloat16), "bal", scatter_dimension=1, tiled=True
        ).astype(jnp.float32),
    )
    key_grad = key_grad[0]
    value_grad = value_grad[0]
    joined_grad = jnp.concatenate(
        [
            norm_backward(query_grad, normal_q, inverse_q),
            norm_backward(key_grad, normal_k, inverse_k),
            value_grad,
        ],
        axis=-1,
    ).astype(jnp.bfloat16)
    normed_grad = lax.dot_general(
        joined_grad, gathered, CONTRACT_LAST, preferred_element_type=jnp.float32
    )
    patch_grad = norm_backward(normed_grad, normal_x, inverse_x).astype(jnp.bfloat16)
    owned = lax.psum_scatter(
        lax.dot_general(normed, joined_grad, CONTRACT_FIRST, preferred_element_type=jnp.float32),
        "fsdp",
        scatter_dimension=0,
        tiled=True,
    )
    total_grad = lax.psum(owned, "bal")
    return (attended.astype(jnp.bfloat16)[None], patch_grad[None], total_grad)


def solution(mesh):
    in_specs = (P("fsdp", "bal", None), P("fsdp", None), P("fsdp", None), P("fsdp", "bal", None))
    out_specs = (P("fsdp", "bal", None), P("fsdp", "bal", None), P("fsdp", None))
    return jax.shard_map(
        per_device, mesh=mesh, in_specs=in_specs, out_specs=out_specs, check_vma=False
    )
```

profile of v0, /device:TPU:16, one launch (start us, length us, event | category | flops | bytes accessed | tf_op | source)
XLA Modules:
  0.0 1705.0 jit_solution(3345752619700770710)
XLA Ops:
  7.2 0.0 copy-start
  7.2 0.0 all-gather.4.cloned.1.call-start
  7.2 0.7 all-gather.4.cloned.1.call-update
  7.9 0.0 reduce-scatter.10.cloned.1.call-start
  8.0 0.7 dynamic-slice_bitcast_fusion
  8.6 1.7 convert_reduce_fusion
  10.3 0.0 copy-start.2
  10.3 2.0 fusion.10
  12.3 0.0 copy-start.1
  12.3 430.4 %all-gather.4.cloned.1.call-done = bf16[6144,192]{1,0:T(8,128)(2,1)} async-done(((bf16[24,192]{1,0:T(8,128)(2,1)}), bf16[6144,192]{1,0:T(8,128)(2,1)}) %all-gather.4.cloned.1.call-update) | async-done | bytes 2359312 | tf_op jit(solution)/shard_map/all_gather | solution.py:30
  442.7 0.0 copy-done
  442.7 3.1 fusion.48
  446.0 12.7 all-gather.1
  458.7 13.1 all-gather
  471.7 0.0 copy-done.2
  471.7 0.3 fusion.51
  472.0 0.0 copy-done.1
  472.1 0.8 fusion.23
  472.8 0.2 fusion.15
  473.1 0.1 fusion.18
  473.2 0.2 copy.7
  473.4 0.7 copy.16
  474.1 0.0 reduce-scatter.10.cloned.1.call-update
  474.1 0.0 reduce-scatter.12.cloned.1.call-start
  474.1 0.1 fusion.17
  474.3 0.2 copy.9
  474.4 0.7 copy.15
  475.1 0.0 reduce-scatter.12.cloned.1.call-update
  475.2 0.0 reduce-scatter.8.cloned.1.call-start
  475.2 29.3 %reduce-scatter.10.cloned.1.call-done = bf16[128,64]{1,0:T(8,128)(2,1)} async-done(((bf16[512,64]{1,0:T(8,128)(2,1)}), bf16[128,64]{1,0:T(8,128)(2,1)}) %reduce-scatter.10.cloned.1.call-update) | async-done | bytes 16400
  504.5 0.8 reshape_bitcast_fusion.1
  505.3 0.1 copy.8
  505.4 0.2 multiply_reduce_fusion
  505.6 34.6 %reduce-scatter.12.cloned.1.call-done = bf16[128,64]{1,0:T(8,128)(2,1)} async-done(((bf16[512,64]{1,0:T(8,128)(2,1)}), bf16[128,64]{1,0:T(8,128)(2,1)}) %reduce-scatter.12.cloned.1.call-update) | async-done | bytes 16400
  540.3 0.8 reshape_bitcast_fusion
  541.1 0.1 copy.10
  541.2 3.8 fusion.34
  545.0 0.0 reduce-scatter.8.cloned.1.call-update
  545.0 3.3 fusion.50
  548.3 2.2 fusion.11
  550.5 1126.6 %reduce-scatter.8.cloned.1.call-done = f32[24,192]{1,0:T(8,128)} async-done(((f32[6144,192]{1,0:T(8,128)}), f32[24,192]{1,0:T(8,128)}) %reduce-scatter.8.cloned.1.call-update) | async-done | bytes 18448 | tf_op jit(solution)/shard_map/reduce_scatter | solution.py:96
  1677.1 21.3 %psum.7 = f32[24,192]{1,0:T(8,128)} all-reduce(f32[24,192]{1,0:T(8,128)} %reduce-scatter.8.cloned.1.call-done), channel_id=1, replica_groups=mesh['bal'=4,'fsdp'=256] {'bal'}, use_global_device_ids=true, to_apply=%region_17.18 | all-reduce | flops 4608 | bytes 36864 | tf_op jit(solution)/shard_map/psum | solution.py:102
  (18 shorter events, 0.2 us)
Async XLA Ops:
  7.2 435.5 %copy-start = (bf16[1,128,6144]{2,1,0:T(8,128)(2,1)S(1)}, bf16[1,128,6144]{2,1,0:T(8,128)(2,1)}, u32[]{:S(2)}) copy-start(bf16[1,128,6144]{2,1,0:T(8,128)(2,1)} %param.4) | copy-start | bytes 4718596
  7.2 435.5 %all-gather.4.cloned.1.call-start = ((), (), s32[]{:S(2)}) async-start(), calls=%async_computation.3 | async-start | bytes 3158016 | tf_op jit(solution)/shard_map/all_gather | solution.py:30
  7.9 496.6 %reduce-scatter.10.cloned.1.call-start = ((), (), s32[]{:S(2)}) async-start(), calls=%async_computation.5 | async-start | bytes 163840
  10.3 461.4 %copy-start.2 = (s32[1,512]{1,0:T(1,128)S(1)}, s32[1,512]{1,0:T(1,128)}, u32[]{:S(2)}) copy-start(s32[1,512]{1,0:T(1,128)} %param.6) | copy-start | bytes 6148
  12.3 459.7 %copy-start.1 = (bf16[1,128,64]{1,2,0:T(8,128)(2,1)S(1)}, bf16[1,128,64]{1,2,0:T(8,128)(2,1)}, u32[]{:S(2)}) copy-start(bf16[1,128,64]{1,2,0:T(8,128)(2,1)} %param.7) | copy-start | bytes 49156
  474.1 66.2 %reduce-scatter.12.cloned.1.call-start = ((), (), s32[]{:S(2)}) async-start(), calls=%async_computation.6 | async-start | bytes 163840
  475.2 1202.0 %reduce-scatter.8.cloned.1.call-start = ((), (), s32[]{:S(2)}) async-start(), calls=%async_computation.4 | async-start | bytes 6316032 | tf_op jit(solution)/shard_map/reduce_scatter | solution.py:96
Sparse Core Ops, SparseCore 0:
  10.8 431.8 all-gather.3
  474.2 30.2 reduce-scatter.9
  508.8 31.4 reduce-scatter.11
  545.1 1131.9 reduce-scatter.7
where the time goes:
time: 1710 us
  waiting for transfers between devices  1620 us (95%)
  blocking collectives  47.1 us (3%)
    reduce_scatter x1, waiting for transfers between devices, per_device(): lax.psum_scatter(lax.dot_general(normed, joined_grad, CONTRACT_FIRST, pre...  1130 us
    all_gather x1, waiting for transfers between devices, per_device(): gathered = lax.all_gather(projection, 'fsdp', axis=0, tiled=True)  430 us
    unnamed x6, waiting for transfers between devices  64.7 us
  transfers between devices with their start and end apart: 4, of which 4 were waited for; matrix products, arithmetic and copies ran while one was open for 1% of the time, Pallas kernels for 0%

commit v1 on v0

v1 whole, which is shorter than its diff:
```python
import functools
import math

import jax
import jax.numpy as jnp
from jax import lax
from jax.experimental import pallas as pl
from jax.experimental.pallas import tpu as pltpu
from jax.sharding import PartitionSpec as P

EPSILON = 1e-06
MESH = pl.DeviceIdType.MESH
F32 = jnp.float32
BF16 = jnp.bfloat16
NT = (((1,), (1,)), ((), ()))
TN = (((0,), (0,)), ((), ()))

D = 6144
HALF = D // 2
ROWS = 128
HD = 64
BLK = 384


def device(z, x, y, c):
    return (y // 2, ((z * 4 + x) * 2 + y % 2) * 2 + c)


def dot(a, b):
    return jnp.dot(a, b, preferred_element_type=F32)


def dot_nt(a, b):
    return lax.dot_general(a, b, NT, preferred_element_type=F32)


def dot_tn(a, b):
    return lax.dot_general(a, b, TN, preferred_element_type=F32)


def kernel(
    x_ref, w_ref, ids_ref, cot_ref,
    out_ref, pg_ref, gw_ref,
    nfull, nall, ntr, stats, zland, wbuf, jpart, jrecv,
    qk_all, v_all, cot_all, jbuf, gbuf, xland, ysend, yland, zsend, zland2, fsend, fland, ngs,
    local_sem, nsem, zs_sem, zr_sem, xs_sem, xr_sem, ys_sem, yr_sem, ws_sem, wr_sem,
    jsem, qs_sem, qr_sem, gsem, gxs_sem, gxr_sem, gys_sem, gyr_sem, gzs_sem, gzr_sem, fs_sem, fr_sem,
):
    h = lax.axis_index("bal")
    f = lax.axis_index("fsdp")
    c = f % 2
    l = (f // 2) % 2
    x = (f // 4) % 4
    z = f // 16
    y = 2 * h + l
    zhalf = z // 8
    zlow = z % 8
    other = device(z, x, y, 1 - c)
    home = zhalf == c
    own = jnp.logical_and(home, z % 4 == h)

    def remote(src, dst, ssem, rsem, dev):
        return pltpu.make_async_remote_copy(
            src_ref=src, dst_ref=dst, send_sem=ssem, recv_sem=rsem, device_id=dev, device_id_type=MESH
        )

    bar = pltpu.get_barrier_semaphore()

    def signal(dev):
        pl.semaphore_signal(bar, inc=1, device_id=dev, device_id_type=MESH)

    for zl in range(8):
        for cs in range(2):
            me = jnp.logical_and(c * 8 + zl == z, c == cs)

            @pl.when(jnp.logical_not(me))
            def _():
                signal(device(c * 8 + zl, x, y, cs))

    @pl.when(own)
    def _():
        for k in range(1, 16):
            signal(device((z + k) % 16, x, y, c))

    @pl.when(jnp.logical_not(own))
    def _():
        signal(device(z, x, 2 * (z % 4) + l, zhalf))

    signal(other)
    for k in range(1, 4):
        signal(device(z, (x + k) % 4, y, c))
    for k in range(1, 8):
        signal(device(z, x, (y + k) % 8, c))
    expected = (
        15 + jnp.where(home, 0, 1) + jnp.where(own, 8, 2) + 1 + 3 + 7
    )

    def norm_body(i, carry):
        rows = pl.ds(pl.multiple_of(i * 16, 16), 16)
        v = x_ref[rows, :].astype(F32)
        mean = jnp.mean(v, axis=-1, keepdims=True)
        cen = v - mean
        inv = lax.rsqrt(jnp.mean(cen * cen, axis=-1, keepdims=True) + EPSILON)
        nfull[rows, :] = (cen * inv).astype(BF16)
        stats[0, rows, :] = jnp.broadcast_to(mean, (16, 128))
        stats[1, rows, :] = jnp.broadcast_to(inv, (16, 128))
        return carry

    lax.fori_loop(0, ROWS // 16, norm_body, 0)
    cot_all[0] = cot_ref[...]

    pl.semaphore_wait(bar, expected)

    zcopies = []
    for k in (8, 7, 9, 6, 10, 5, 11, 4, 12, 3, 13, 2, 14, 1, 15):
        cp = remote(w_ref, zland.at[zlow, c], zs_sem.at[k], zr_sem.at[zlow, c], device((z + k) % 16, x, y, zhalf))
        cp.start()
        zcopies.append(cp)
    zcross = remote(w_ref, zland.at[zlow, c], zs_sem.at[0], zr_sem.at[zlow, c], other)

    @pl.when(jnp.logical_not(home))
    def _():
        zcross.start()

    @pl.when(home)
    def _():
        zland[zlow, c] = w_ref[...]

    mine = pl.ds(pl.multiple_of(c * ROWS, ROWS), ROWS)
    ncopy = remote(
        nfull.at[:, pl.ds(pl.multiple_of((1 - c) * HALF, HALF), HALF)], nall.at[mine], nsem.at[0], nsem.at[1], other
    )
    ncopy.start()
    nlocal = pltpu.make_async_copy(
        nfull.at[:, pl.ds(pl.multiple_of(c * HALF, HALF), HALF)], nall.at[mine], local_sem
    )
    nlocal.start()
    ccopies = []
    for k in range(1, 4):
        cp = remote(cot_all.at[0], cot_all.at[4 - k], qs_sem.at[2, k], qr_sem.at[2, k], device(z, x, (y + 2 * k) % 8, c))
        cp.start()
        ccopies.append(cp)
    nlocal.wait()
    ncopy.wait()

    def tr_body(i, carry):
        col = pl.ds(pl.multiple_of(i * BLK, BLK), BLK)
        ntr[col, :] = nall[:, col].T
        return carry

    lax.fori_loop(0, 8, tr_body, 0)

    xcopies = []
    for zz in range(4):
        halves = []
        for zl in (zz, zz + 4):
            for cs in range(2):
                me = jnp.logical_and(c * 8 + zl == z, c == cs)

                @pl.when(jnp.logical_not(me))
                def _():
                    remote(w_ref, zland.at[zl, cs], zs_sem.at[0], zr_sem.at[zl, cs], other).wait_recv()

            halves.append(
                jnp.concatenate([zland[zl, 0].astype(F32), zland[zl, 1].astype(F32)], axis=0)
            )
        a, b = halves
        wbuf[c, zz, 0, x, l] = a[:, :128].astype(BF16)
        wbuf[c, zz, 1, x, l] = b[:, :128].astype(BF16)
        wbuf[c, zz, 2, x, l] = jnp.concatenate([a[:, 128:], b[:, 128:]], axis=1).astype(BF16)
        piece = wbuf.at[c, zz, :, x, l]
        for k in (2, 1, 3):
            cp = remote(piece, piece, xs_sem.at[zz, k], xr_sem.at[zz, k], device(z, (x + k) % 4, y, c))
            cp.start()
            xcopies.append(cp)

    order = (0, 2, 1, 3)
    ycopies = {}
    for zz in order:
        for k in range(1, 4):
            src = wbuf.at[c, zz, :, (x + 4 - k) % 4, l]
            remote(src, src, xs_sem.at[zz, k], xr_sem.at[zz, k], other).wait_recv()
        piece = wbuf.at[c, zz, :, :, l]
        step = 1 if zz < 2 else 7
        cp = remote(piece, piece, ys_sem.at[zz], yr_sem.at[zz], device(z, x, (y + step) % 8, c))
        cp.start()
        ycopies[zz] = cp

    wcopies = []
    acc_a = jnp.zeros((2 * ROWS, 256), F32)
    acc_b = jnp.zeros((2 * ROWS, 256), F32)
    for zz in order:
        dst = wbuf.at[c, zz, :, :, 1 - l]
        remote(dst, dst, ys_sem.at[zz], yr_sem.at[zz], other).wait_recv()
        cp = remote(wbuf.at[c, zz], wbuf.at[c, zz], ws_sem.at[zz], wr_sem.at[zz], other)
        cp.start()
        wcopies.append(cp)
        w0 = wbuf[c, zz, 0].reshape(BLK, 128)
        w1 = wbuf[c, zz, 1].reshape(BLK, 128)
        w2 = wbuf[c, zz, 2].reshape(BLK, 128)
        na = nall[:, zz * BLK : (zz + 1) * BLK]
        nb = nall[:, (zz + 4) * BLK : (zz + 5) * BLK]
        acc_a += dot(na, jnp.concatenate([w0, w2], axis=1))
        acc_b += dot(nb, jnp.concatenate([w1, w2], axis=1))
    jq = acc_a[:, :128] + acc_b[:, :128]
    jv = acc_a[:, 128:192] + acc_b[:, 192:]
    for i in range(2):
        jpart[i, :, :128] = jq[i * ROWS : (i + 1) * ROWS]
        jpart[i, :, 128:] = jv[i * ROWS : (i + 1) * ROWS]
    jcopy = remote(jpart.at[1 - c], jrecv, jsem.at[0], jsem.at[1], other)
    jcopy.start()
    jcopy.wait_recv()
    joined = jpart[c] + jrecv[...]

    def norm_rows(values):
        centred = values - jnp.mean(values, axis=-1, keepdims=True)
        inverse = lax.rsqrt(jnp.mean(centred * centred, axis=-1, keepdims=True) + EPSILON)
        return centred * inverse, inverse

    normal_q, inverse_q = norm_rows(joined[:, :HD])
    normal_k, inverse_k = norm_rows(joined[:, HD : 2 * HD])
    value = joined[:, 2 * HD :]
    qk_all[0] = jnp.concatenate([normal_q, normal_k], axis=1).astype(BF16)
    v_all[0] = jnp.concatenate([value[:64], value[64:]], axis=1).astype(BF16)
    qcopies = []
    for k in (2, 1, 3):
        for i, buf in enumerate((qk_all, v_all)):
            cp = remote(
                buf.at[0], buf.at[4 - k], qs_sem.at[i, k], qr_sem.at[i, k], device(z, x, (y + 2 * k) % 8, c)
            )
            cp.start()
            qcopies.append(cp)
    id_rows = [
        ids_ref[:, pl.ds(pl.multiple_of(((h + r) % 4) * ROWS, ROWS), ROWS)].astype(F32) for r in range(4)
    ]
    id_row = jnp.concatenate(id_rows, axis=1)
    id_cols = [jnp.broadcast_to(r, (128, 128)).T[:, :1] for r in id_rows]
    for cp in ccopies + qcopies:
        cp.wait_recv()

    qs, ks, vs, cots = [], [], [], []
    for r in range(4):
        both = qk_all[r].astype(F32)
        qs.append(both[:, :HD].astype(BF16))
        ks.append(both[:, HD:].astype(BF16))
        packed = v_all[r].astype(F32)
        vs.append(jnp.concatenate([packed[:, :HD], packed[:, HD:]], axis=0).astype(BF16))
        cots.append(cot_all[r].astype(F32))
    k_whole = jnp.concatenate(ks, axis=0)
    v_whole = jnp.concatenate(vs, axis=0)
    factor = 1.0 / math.sqrt(HD)
    key_grad = jnp.zeros((ROWS, HD), F32)
    value_grad = jnp.zeros((ROWS, HD), F32)
    query_grad = None
    for r in range(4):
        scores = dot_nt(qs[r], k_whole) * factor
        expo = jnp.where(id_cols[r] == id_row, jnp.exp(scores), 0.0)
        denom = jnp.sum(expo, axis=-1, keepdims=True)
        probs = expo.astype(BF16)
        attended = dot(probs, v_whole) / denom
        scaled = (cots[r] / denom).astype(BF16)
        correction = jnp.sum(cots[r] * attended, axis=-1, keepdims=True) / denom
        if r == 0:
            out_ref[...] = attended.astype(BF16)
            pgrad = dot_nt(scaled, v_whole)
            sgrad = (probs.astype(F32) * (pgrad - correction)).astype(BF16)
            query_grad = dot(sgrad, k_whole) * factor
            sgrad = sgrad[:, :ROWS]
        else:
            pgrad = dot_nt(scaled, vs[0])
            sgrad = (probs[:, :ROWS].astype(F32) * (pgrad - correction)).astype(BF16)
        key_grad += dot_tn(sgrad, qs[r])
        value_grad += dot_tn(probs[:, :ROWS], scaled)
    key_grad = key_grad * factor

    def norm_backward(upstream, normal, inverse):
        shifted = upstream - jnp.mean(upstream, axis=-1, keepdims=True)
        return inverse * (shifted - normal * jnp.mean(upstream * normal, axis=-1, keepdims=True))

    zero = jnp.zeros((ROWS, HD), F32)
    jbuf[c, 0] = jnp.concatenate(
        [norm_backward(query_grad, normal_q, inverse_q), norm_backward(key_grad, normal_k, inverse_k)], axis=1
    ).astype(BF16)
    jbuf[c, 1] = jnp.concatenate([value_grad, zero], axis=1).astype(BF16)
    jbuf[c, 2] = jnp.concatenate([zero, value_grad], axis=1).astype(BF16)
    gcopy = remote(jbuf.at[c], jbuf.at[c], gsem.at[0], gsem.at[1], other)
    gcopy.start()
    theirs = jbuf.at[1 - c]
    remote(theirs, theirs, gsem.at[0], gsem.at[1], other).wait_recv()

    jplanes = [jnp.concatenate([jbuf[0, i], jbuf[1, i]], axis=0) for i in range(3)]
    ja = jnp.concatenate([jplanes[0], jplanes[1]], axis=1)
    jb = jnp.concatenate([jplanes[0], jplanes[2]], axis=1)
    gxcopies = []
    for t in range(4):
        zz = (h + t) % 4
        ga = dot(ntr[pl.ds(pl.multiple_of(zz * BLK, BLK), BLK), :], ja)
        gb = dot(ntr[pl.ds(pl.multiple_of((zz + 4) * BLK, BLK), BLK), :], jb)
        gbuf[zz, 0] = ga[:, :128].astype(BF16).reshape(4, 2, 48, 128)
        gbuf[zz, 1] = gb[:, :128].astype(BF16).reshape(4, 2, 48, 128)
        gbuf[zz, 2] = (ga[:, 128:] + gb[:, 128:]).astype(BF16).reshape(4, 2, 48, 128)
        for k in (2, 1, 3):
            cp = remote(
                gbuf.at[zz, :, (x + k) % 4], xland.at[t, k - 1], gxs_sem.at[t, k], gxr_sem.at[t, k],
                device(z, (x + k) % 4, y, c),
            )
            cp.start()
            gxcopies.append(cp)

    for cp in wcopies:
        cp.wait_send()
    for zz in order:
        dst = wbuf.at[1 - c, zz]
        remote(dst, dst, ws_sem.at[zz], wr_sem.at[zz], other).wait_recv()
    jown_a = jnp.concatenate([jbuf[c, 0], jbuf[c, 1]], axis=1)
    jown_b = jnp.concatenate([jbuf[c, 0], jbuf[c, 2]], axis=1)

    def pg_first(i, carry):
        s1, s2 = carry
        half = i // 4
        zz = i % 4
        w2 = wbuf[half, zz, 2].reshape(BLK, 128)
        mean = stats[0]
        inv = stats[1]
        for ab in range(2):
            wab = wbuf[half, zz, ab].reshape(BLK, 128)
            ng = dot_nt(jown_a if ab == 0 else jown_b, jnp.concatenate([wab, w2], axis=1))
            base = (half * 8 + zz + 4 * ab) * BLK
            for j in range(3):
                col = pl.ds(pl.multiple_of(base + j * 128, 128), 128)
                g = ng[:, j * 128 : (j + 1) * 128]
                hx = (x_ref[:, col].astype(F32) - mean) * inv
                ngs[:, col] = g
                s1 = s1 + g
                s2 = s2 + g * hx
        return s1, s2

    s1 = jnp.zeros((ROWS, 128), F32)
    s2 = s1
    for i in range(8):
        s1, s2 = pg_first(i, (s1, s2))
    m1 = jnp.broadcast_to(jnp.sum(s1, axis=-1, keepdims=True) * (1.0 / D), (ROWS, 128))
    m2 = jnp.broadcast_to(jnp.sum(s2, axis=-1, keepdims=True) * (1.0 / D), (ROWS, 128))
    stats[2] = m1
    stats[3] = m2

    gycopies = []
    for t in range(4):
        zz = (h + t) % 4
        total = gbuf[zz, :, x].astype(F32)
        for k in range(1, 4):
            dst = xland.at[t, k - 1]
            remote(dst, dst, gxs_sem.at[t, k], gxr_sem.at[t, k], other).wait_recv()
            total = total + xland[t, k - 1].astype(F32)
        ysend[t] = total.astype(BF16)
        for e in range(2):
            if t == 0 and e == 0:
                continue
            lt = (l + e) % 2
            yt = 2 * zz + lt
            slot = (y - yt + 8) % 8
            cp = remote(
                ysend.at[t, :, lt], yland.at[slot], gys_sem.at[t, e], gyr_sem.at[slot], device(z, x, yt, c)
            )
            cp.start()
            gycopies.append(cp)

    total = ysend[0, :, l].astype(F32)
    for k in range(1, 8):
        dst = yland.at[k]
        remote(dst, dst, gys_sem.at[0, 1], gyr_sem.at[k], other).wait_recv()
        total = total + yland[k].astype(F32)
    tb = total.astype(BF16)
    zsend[0] = tb[0]
    zsend[1] = tb[2]
    zsend[2] = tb[1]
    zsend[3] = tb[2]
    gzcopies = []
    for i in range(2):
        zt = c * 8 + h + 4 * i
        cp = remote(
            zsend.at[pl.ds(2 * i, 2)], zland2.at[z], gzs_sem.at[i], gzr_sem.at[z], device(zt, x, y, c)
        )
        gzcopies.append((zt, cp))

        @pl.when(zt != z)
        def _():
            cp.start()

    def pg_second(i, carry):
        mean = stats[0]
        inv = stats[1]
        m1 = stats[2]
        m2 = stats[3]
        for j in range(3):
            col = pl.ds(pl.multiple_of(i * BLK + j * 128, 128), 128)
            hx = (x_ref[:, col].astype(F32) - mean) * inv
            pg_ref[:, col] = (inv * (ngs[:, col] - m1 - hx * m2)).astype(BF16)
        return carry

    lax.fori_loop(0, 16, pg_second, 0)

    fcopies = []
    for dh in range(4):
        for dc in range(2):
            if dh == 0 and dc == 0:
                continue
            ct = (c + dc) % 2
            fcopies.append(
                remote(
                    fsend.at[ct], fland, fs_sem.at[2 * dh + dc], fr_sem, device(z, x, (y + 2 * dh) % 8, ct)
                )
            )

    @pl.when(own)
    def _():
        second = zlow // 4
        total = zsend[pl.ds(2 * second, 2)].astype(F32)
        for k in (1, 15, 2, 14, 3, 13, 4, 12, 5, 11, 6, 10, 7, 9, 8):
            dst = zland2.at[(z + k) % 16]
            remote(dst, dst, gzs_sem.at[0], gzr_sem.at[(z + k) % 16], other).wait_recv()
            total = total + zland2[(z + k) % 16].astype(F32)
        pair = total[1]
        mine_v = jnp.where(second == 0, pair[:, :HD], pair[:, HD:])
        whole = jnp.concatenate([total[0], mine_v], axis=1)
        fsend[0] = whole[:24]
        fsend[1] = whole[24:]
        for cp in fcopies:
            cp.start()
        gw_ref[...] = fsend[c]
        for cp in fcopies:
            cp.wait_send()

    @pl.when(jnp.logical_not(own))
    def _():
        remote(fland, fland, fs_sem.at[0], fr_sem, other).wait_recv()
        gw_ref[...] = fland[...]

    for cp in zcopies:
        cp.wait_send()

    @pl.when(jnp.logical_not(home))
    def _():
        zcross.wait_send()

    jcopy.wait_send()
    gcopy.wait_send()
    for cp in xcopies + list(ycopies.values()) + ccopies + qcopies + gxcopies + gycopies:
        cp.wait_send()
    for zt, cp in gzcopies:

        @pl.when(zt != z)
        def _():
            cp.wait_send()


def per_device(patches, projection, image_ids, cotangent):
    dma = pltpu.SemaphoreType.DMA
    vmem = pl.BlockSpec(memory_space=pltpu.VMEM)
    scratch = [
        pltpu.VMEM((ROWS, D), BF16),
        pltpu.VMEM((2 * ROWS, HALF), BF16),
        pltpu.VMEM((HALF, 2 * ROWS), BF16),
        pltpu.VMEM((4, ROWS, 128), F32),
        pltpu.VMEM((8, 2, 24, 192), BF16),
        pltpu.VMEM((2, 4, 3, 4, 2, 48, 128), BF16),
        pltpu.VMEM((2, ROWS, 192), F32),
        pltpu.VMEM((ROWS, 192), F32),
        pltpu.VMEM((4, ROWS, 128), BF16),
        pltpu.VMEM((4, 64, 128), BF16),
        pltpu.VMEM((4, ROWS, HD), BF16),
        pltpu.VMEM((2, 3, ROWS, 128), BF16),
        pltpu.VMEM((4, 3, 4, 2, 48, 128), BF16),
        pltpu.VMEM((4, 3, 3, 2, 48, 128), BF16),
        pltpu.VMEM((4, 3, 2, 48, 128), BF16),
        pltpu.VMEM((8, 3, 48, 128), BF16),
        pltpu.VMEM((4, 48, 128), BF16),
        pltpu.VMEM((16, 2, 48, 128), BF16),
        pltpu.VMEM((2, 24, 192), F32),
        pltpu.VMEM((24, 192), F32),
        pltpu.VMEM((ROWS, D), F32),
        dma,
        dma((2,)),
        dma((16,)), dma((8, 2)),
        dma((4, 4)), dma((4, 4)),
        dma((4,)), dma((4,)),
        dma((4,)), dma((4,)),
        dma((2,)),
        dma((3, 4)), dma((3, 4)),
        dma((2,)),
        dma((4, 4)), dma((4, 4)),
        dma((4, 2)), dma((8,)),
        dma((2,)), dma((16,)),
        dma((8,)), dma,
    ]
    out, pg, gw = pl.pallas_call(
        kernel,
        out_shape=(
            jax.ShapeDtypeStruct((ROWS, HD), BF16),
            jax.ShapeDtypeStruct((ROWS, D), BF16),
            jax.ShapeDtypeStruct((24, 192), F32),
        ),
        in_specs=[vmem] * 4,
        out_specs=(vmem,) * 3,
        scratch_shapes=scratch,
        compiler_params=pltpu.CompilerParams(
            collective_id=0, has_side_effects=True, vmem_limit_bytes=48 * 2**20
        ),
        name="head",
    )(patches[0], projection, image_ids, cotangent[0])
    return out[None], pg[None], gw


def solution(mesh):
    in_specs = (P("fsdp", "bal", None), P("fsdp", None), P("fsdp", None), P("fsdp", "bal", None))
    out_specs = (P("fsdp", "bal", None), P("fsdp", "bal", None), P("fsdp", None))
    return jax.shard_map(
        per_device, mesh=mesh, in_specs=in_specs, out_specs=out_specs, check_vma=False
    )
```

time: 1710 us -> 99.8 us (0.06)
  the two profiles are of different devices: /device:TPU:16 before, /device:TPU:65 now
where the time goes in v1:
time: 99.8 us; the launch traced here: 99.5 us
  Pallas kernels  92.8 us (93%)
  local copies, waits for them, and re-layouts  6.07 us (6%)
    pallas_call x1, Pallas kernels, per_device(): pl.pallas_call(kernel, out_shape=(jax.ShapeDtypeStruct((ROWS, HD), BF16),...  92.8 us
    unnamed x10, local copies, waits for them, and re-layouts  6.07 us

profile of v1, /device:TPU:65, one launch (start us, length us, event | category | flops | bytes accessed | tf_op | source)
XLA Modules:
  0.0 99.5 jit_solution(9418386453567279513)
XLA Ops:
  0.6 0.8 copy.7
  1.5 0.0 copy-start
  1.5 1.4 %copy-done = bf16[1,128,6144]{2,1,0:T(8,128)(2,1)S(1)} copy-done((bf16[1,128,6144]{2,1,0:T(8,128)(2,1)S(1)}, bf16[1,128,6144]{2,1,0:T(8,128)(2,1)}, u32[]{:S(2)}) %copy-start) | copy-done | bytes 1572888
  2.9 0.0 copy-start.1
  2.9 0.7 copy-done.1
  3.6 0.0 copy-start.2
  3.6 0.7 copy-done.2
  4.3 92.8 %head.1 = (bf16[128,64]{1,0:T(8,128)(2,1)S(1)}, bf16[128,6144]{1,0:T(8,128)(2,1)S(1)}, f32[24,192]{1,0:T(8,128)S(1)}) custom-call(bf16[128,6144]{1,0:T(8,128)(2,1)S(1)} %bitcast.4, bf16[24,192]{1,0:T(8,128)(2,1)S(1)} %copy-done.1, s32[1,512]{1,0:T(1,128)S(1)} %copy-done.2, bf16[128,64]{1,0:T(8,128)(2,1)S(1)} %bitcast.6), custom_call_target="tpu_custom_call" | custom-call | tf_op jit(solution)/shard_map/head/pallas_call | solution.py:496
  97.1 0.7 copy.8
  97.8 1.1 %copy.11 = bf16[1,128,6144]{2,1,0:T(8,128)(2,1)} copy(bf16[1,128,6144]{2,1,0:T(8,128)(2,1)S(1)} %bitcast.5) | data formatting | bytes 3145728
  98.9 0.6 copy.12
Async XLA Ops:
  1.5 1.4 %copy-start = (bf16[1,128,6144]{2,1,0:T(8,128)(2,1)S(1)}, bf16[1,128,6144]{2,1,0:T(8,128)(2,1)}, u32[]{:S(2)}) copy-start(bf16[1,128,6144]{2,1,0:T(8,128)(2,1)} %param.4) | copy-start | bytes 4718596
  2.9 0.7 copy-start.1
  3.6 0.7 copy-start.2

commit v2 on v1

--- a/solution.py
+++ b/solution.py
@@ -39,9 +39,9 @@
 
 
 def kernel(
-    x_ref, w_ref, ids_ref, cot_ref,
+    x_hbm, w_hbm, ids_hbm, cot_hbm,
     out_ref, pg_ref, gw_ref,
-    nfull, nall, ntr, stats, zland, wbuf, jpart, jrecv,
+    x_ref, w_ref, ids_ref, wpack, relay, msend, in_sem, nfull, nall, ntr, stats, zland, wbuf, jpart, jrecv,
     qk_all, v_all, cot_all, jbuf, gbuf, xland, ysend, yland, zsend, zland2, fsend, fland, ngs,
     local_sem, nsem, zs_sem, zr_sem, xs_sem, xr_sem, ys_sem, yr_sem, ws_sem, wr_sem,
     jsem, qs_sem, qr_sem, gsem, gxs_sem, gxr_sem, gys_sem, gyr_sem, gzs_sem, gzr_sem, fs_sem, fr_sem,
@@ -57,13 +57,22 @@
     zlow = z % 8
     other = device(z, x, y, 1 - c)
     home = zhalf == c
-    own = jnp.logical_and(home, z % 4 == h)
+    own = jnp.logical_and(home, zlow // 2 == h)
 
     def remote(src, dst, ssem, rsem, dev):
         return pltpu.make_async_remote_copy(
             src_ref=src, dst_ref=dst, send_sem=ssem, recv_sem=rsem, device_id=dev, device_id_type=MESH
         )
 
+    loads = [
+        pltpu.make_async_copy(x_hbm.at[pl.ds(i * 32, 32)], x_ref.at[pl.ds(i * 32, 32)], in_sem.at[i]) for i in range(4)
+    ]
+    w_load = pltpu.make_async_copy(w_hbm, w_ref, in_sem.at[4])
+    ids_load = pltpu.make_async_copy(ids_hbm, ids_ref, in_sem.at[5])
+    cot_load = pltpu.make_async_copy(cot_hbm, cot_all.at[0], in_sem.at[6])
+    for cp in [w_load, *loads, ids_load, cot_load]:
+        cp.start()
+
     bar = pltpu.get_barrier_semaphore()
 
     def signal(dev):
@@ -84,7 +93,7 @@
 
     @pl.when(jnp.logical_not(own))
     def _():
-        signal(device(z, x, 2 * (z % 4) + l, zhalf))
+        signal(device(z, x, 2 * (zlow // 2) + l, zhalf))
 
     signal(other)
     for k in range(1, 4):
@@ -106,17 +115,27 @@
         stats[1, rows, :] = jnp.broadcast_to(inv, (16, 128))
         return carry
 
-    lax.fori_loop(0, ROWS // 16, norm_body, 0)
-    cot_all[0] = cot_ref[...]
+    w_load.wait()
+    wf = w_ref[...].astype(F32)
+    wv = wf[:, 128:]
+    wpack[...] = jnp.concatenate(
+        [wf[:, :128], jnp.concatenate([wv[:16], jnp.concatenate([wv[16:], jnp.zeros((8, HD), F32)], axis=0)], axis=1)],
+        axis=0,
+    ).astype(BF16)
+    for i in range(4):
+        loads[i].wait()
+        lax.fori_loop(2 * i, 2 * i + 2, norm_body, 0)
+    ids_load.wait()
+    cot_load.wait()
 
     pl.semaphore_wait(bar, expected)
 
     zcopies = []
-    for k in (8, 7, 9, 6, 10, 5, 11, 4, 12, 3, 13, 2, 14, 1, 15):
-        cp = remote(w_ref, zland.at[zlow, c], zs_sem.at[k], zr_sem.at[zlow, c], device((z + k) % 16, x, y, zhalf))
+    for k in (1, 15, 2, 14, 3, 13, 4, 12, 5, 11, 6, 10, 7, 9, 8):
+        cp = remote(wpack, zland.at[zlow, c], zs_sem.at[k], zr_sem.at[zlow, c], device((z + k) % 16, x, y, zhalf))
         cp.start()
         zcopies.append(cp)
-    zcross = remote(w_ref, zland.at[zlow, c], zs_sem.at[0], zr_sem.at[zlow, c], other)
+    zcross = remote(wpack, zland.at[zlow, c], zs_sem.at[0], zr_sem.at[zlow, c], other)
 
     @pl.when(jnp.logical_not(home))
     def _():
@@ -124,7 +143,7 @@
 
     @pl.when(home)
     def _():
-        zland[zlow, c] = w_ref[...]
+        zland[zlow, c] = wpack[...]
 
     mine = pl.ds(pl.multiple_of(c * ROWS, ROWS), ROWS)
     ncopy = remote(
@@ -150,58 +169,84 @@
 
     lax.fori_loop(0, 8, tr_body, 0)
 
+    near = []
+    for zz in range(4):
+        gap = (z // 2 + 8 - (4 * c + zz)) % 8
+        near.append(jnp.minimum(gap, 8 - gap) * 4 + zz)
+    ranks = [sum((near[j] < near[i]).astype(jnp.int32) for j in range(4) if j != i) for i in range(4)]
+    order = [sum(jnp.where(ranks[i] == t, i, 0) for i in range(4)) for t in range(4)]
+
+    def shard(zl, cs):
+        me = jnp.logical_and(c * 8 + zl == z, c == cs)
+
+        @pl.when(jnp.logical_not(me))
+        def _():
+            remote(wpack, zland.at[zl, cs], zs_sem.at[0], zr_sem.at[zl, cs], other).wait_recv()
+
+        return zland[zl, cs].astype(F32)
+
     xcopies = []
-    for zz in range(4):
-        halves = []
-        for zl in (zz, zz + 4):
-            for cs in range(2):
-                me = jnp.logical_and(c * 8 + zl == z, c == cs)
-
-                @pl.when(jnp.logical_not(me))
-                def _():
-                    remote(w_ref, zland.at[zl, cs], zs_sem.at[0], zr_sem.at[zl, cs], other).wait_recv()
-
-            halves.append(
-                jnp.concatenate([zland[zl, 0].astype(F32), zland[zl, 1].astype(F32)], axis=0)
+    ycopies = []
+    wcopies = []
+
+    def along_x(t):
+        zz = order[t]
+        heads, values = [], []
+        for zl in (2 * zz, 2 * zz + 1):
+            parts = [shard(zl, 0), shard(zl, 1)]
+            heads.append(jnp.concatenate([p[:24] for p in parts], axis=0))
+            values.append(
+                jnp.concatenate([q for p in parts for q in (p[24:, :HD], p[24:32, HD:])], axis=0)
             )
-        a, b = halves
-        wbuf[c, zz, 0, x, l] = a[:, :128].astype(BF16)
-        wbuf[c, zz, 1, x, l] = b[:, :128].astype(BF16)
-        wbuf[c, zz, 2, x, l] = jnp.concatenate([a[:, 128:], b[:, 128:]], axis=1).astype(BF16)
+        wbuf[c, zz, 0, x, l] = heads[0].astype(BF16)
+        wbuf[c, zz, 1, x, l] = heads[1].astype(BF16)
+        wbuf[c, zz, 2, x, l] = jnp.concatenate(values, axis=1).astype(BF16)
         piece = wbuf.at[c, zz, :, x, l]
         for k in (2, 1, 3):
-            cp = remote(piece, piece, xs_sem.at[zz, k], xr_sem.at[zz, k], device(z, (x + k) % 4, y, c))
+            cp = remote(piece, piece, xs_sem.at[t, k], xr_sem.at[t, k], device(z, (x + k) % 4, y, c))
             cp.start()
             xcopies.append(cp)
 
-    order = (0, 2, 1, 3)
-    ycopies = {}
-    for zz in order:
+    def along_y(t):
+        zz = order[t]
         for k in range(1, 4):
             src = wbuf.at[c, zz, :, (x + 4 - k) % 4, l]
-            remote(src, src, xs_sem.at[zz, k], xr_sem.at[zz, k], other).wait_recv()
+            remote(src, src, xs_sem.at[t, k], xr_sem.at[t, k], other).wait_recv()
         piece = wbuf.at[c, zz, :, :, l]
-        step = 1 if zz < 2 else 7
-        cp = remote(piece, piece, ys_sem.at[zz], yr_sem.at[zz], device(z, x, (y + step) % 8, c))
+        cp = remote(piece, piece, ys_sem.at[t], yr_sem.at[t], device(z, x, (y + (1, 7)[t % 2]) % 8, c))
         cp.start()
-        ycopies[zz] = cp
-
-    wcopies = []
-    acc_a = jnp.zeros((2 * ROWS, 256), F32)
-    acc_b = jnp.zeros((2 * ROWS, 256), F32)
-    for zz in order:
+        ycopies.append(cp)
+
+    def multiply(t, accs):
+        zz = order[t]
         dst = wbuf.at[c, zz, :, :, 1 - l]
-        remote(dst, dst, ys_sem.at[zz], yr_sem.at[zz], other).wait_recv()
-        cp = remote(wbuf.at[c, zz], wbuf.at[c, zz], ws_sem.at[zz], wr_sem.at[zz], other)
+        remote(dst, dst, ys_sem.at[t], yr_sem.at[t], other).wait_recv()
+        cp = remote(wbuf.at[c, zz], wbuf.at[c, zz], ws_sem.at[t], wr_sem.at[zz], other)
         cp.start()
         wcopies.append(cp)
         w0 = wbuf[c, zz, 0].reshape(BLK, 128)
         w1 = wbuf[c, zz, 1].reshape(BLK, 128)
         w2 = wbuf[c, zz, 2].reshape(BLK, 128)
-        na = nall[:, zz * BLK : (zz + 1) * BLK]
-        nb = nall[:, (zz + 4) * BLK : (zz + 5) * BLK]
-        acc_a += dot(na, jnp.concatenate([w0, w2], axis=1))
-        acc_b += dot(nb, jnp.concatenate([w1, w2], axis=1))
+        na = nall[:, pl.ds(pl.multiple_of(2 * zz * BLK, BLK), BLK)]
+        nb = nall[:, pl.ds(pl.multiple_of((2 * zz + 1) * BLK, BLK), BLK)]
+        return (
+            accs[0] + dot(na, jnp.concatenate([w0, w2], axis=1)),
+            accs[1] + dot(nb, jnp.concatenate([w1, w2], axis=1)),
+        )
+
+    accs = (jnp.zeros((2 * ROWS, 256), F32), jnp.zeros((2 * ROWS, 256), F32))
+    along_x(0)
+    along_x(1)
+    along_x(2)
+    along_y(0)
+    along_x(3)
+    along_y(1)
+    along_y(2)
+    accs = multiply(0, accs)
+    along_y(3)
+    for t in range(1, 4):
+        accs = multiply(t, accs)
+    acc_a, acc_b = accs
     jq = acc_a[:, :128] + acc_b[:, :128]
     jv = acc_a[:, 128:192] + acc_b[:, 192:]
     for i in range(2):
@@ -245,7 +290,7 @@
         ks.append(both[:, HD:].astype(BF16))
         packed = v_all[r].astype(F32)
         vs.append(jnp.concatenate([packed[:, :HD], packed[:, HD:]], axis=0).astype(BF16))
-        cots.append(cot_all[r].astype(F32))
+        cots.append(cot_all[r].astype(F32).T)
     k_whole = jnp.concatenate(ks, axis=0)
     v_whole = jnp.concatenate(vs, axis=0)
     factor = 1.0 / math.sqrt(HD)
@@ -261,7 +306,7 @@
         scaled = (cots[r] / denom).astype(BF16)
         correction = jnp.sum(cots[r] * attended, axis=-1, keepdims=True) / denom
         if r == 0:
-            out_ref[...] = attended.astype(BF16)
+            out_ref[...] = attended.T.astype(BF16)
             pgrad = dot_nt(scaled, v_whole)
             sgrad = (probs.astype(F32) * (pgrad - correction)).astype(BF16)
             query_grad = dot(sgrad, k_whole) * factor
@@ -292,24 +337,35 @@
     ja = jnp.concatenate([jplanes[0], jplanes[1]], axis=1)
     jb = jnp.concatenate([jplanes[0], jplanes[2]], axis=1)
     gxcopies = []
-    for t in range(4):
+    order_t = (2, 1, 3, 0)
+    toward = {t: (1, 3)[i % 2] for i, t in enumerate(order_t)}
+    for t in order_t:
         zz = (h + t) % 4
-        ga = dot(ntr[pl.ds(pl.multiple_of(zz * BLK, BLK), BLK), :], ja)
-        gb = dot(ntr[pl.ds(pl.multiple_of((zz + 4) * BLK, BLK), BLK), :], jb)
+        ga = dot(ntr[pl.ds(pl.multiple_of(2 * zz * BLK, BLK), BLK), :], ja)
+        gb = dot(ntr[pl.ds(pl.multiple_of((2 * zz + 1) * BLK, BLK), BLK), :], jb)
         gbuf[zz, 0] = ga[:, :128].astype(BF16).reshape(4, 2, 48, 128)
         gbuf[zz, 1] = gb[:, :128].astype(BF16).reshape(4, 2, 48, 128)
         gbuf[zz, 2] = (ga[:, 128:] + gb[:, 128:]).astype(BF16).reshape(4, 2, 48, 128)
-        for k in (2, 1, 3):
-            cp = remote(
-                gbuf.at[zz, :, (x + k) % 4], xland.at[t, k - 1], gxs_sem.at[t, k], gxr_sem.at[t, k],
-                device(z, (x + k) % 4, y, c),
-            )
+        near_x, back_x = (x + toward[t]) % 4, (x + 4 - toward[t]) % 4
+        for cp in (
+            remote(gbuf.at[zz, :, (x + 2) % 4], relay.at[t], gxs_sem.at[t, 0], gxr_sem.at[t, 0], device(z, near_x, y, c)),
+            remote(gbuf.at[zz, :, back_x], xland.at[t, 0], gxs_sem.at[t, 1], gxr_sem.at[t, 1], device(z, back_x, y, c)),
+        ):
             cp.start()
             gxcopies.append(cp)
 
+    def merge(t):
+        zz = (h + t) % 4
+        near_x = (x + toward[t]) % 4
+        remote(relay.at[t], relay.at[t], gxs_sem.at[t, 0], gxr_sem.at[t, 0], other).wait_recv()
+        msend[t] = (gbuf[zz, :, near_x].astype(F32) + relay[t].astype(F32)).astype(BF16)
+        cp = remote(msend.at[t], xland.at[t, 1], gxs_sem.at[t, 2], gxr_sem.at[t, 2], device(z, near_x, y, c))
+        cp.start()
+        gxcopies.append(cp)
+
     for cp in wcopies:
         cp.wait_send()
-    for zz in order:
+    for zz in range(4):
         dst = wbuf.at[1 - c, zz]
         remote(dst, dst, ws_sem.at[zz], wr_sem.at[zz], other).wait_recv()
     jown_a = jnp.concatenate([jbuf[c, 0], jbuf[c, 1]], axis=1)
@@ -325,7 +381,7 @@
         for ab in range(2):
             wab = wbuf[half, zz, ab].reshape(BLK, 128)
             ng = dot_nt(jown_a if ab == 0 else jown_b, jnp.concatenate([wab, w2], axis=1))
-            base = (half * 8 + zz + 4 * ab) * BLK
+            base = (half * 8 + 2 * zz + ab) * BLK
             for j in range(3):
                 col = pl.ds(pl.multiple_of(base + j * 128, 128), 128)
                 g = ng[:, j * 128 : (j + 1) * 128]
@@ -339,19 +395,21 @@
     s2 = s1
     for i in range(8):
         s1, s2 = pg_first(i, (s1, s2))
+        if i % 2 == 1:
+            merge(order_t[i // 2])
     m1 = jnp.broadcast_to(jnp.sum(s1, axis=-1, keepdims=True) * (1.0 / D), (ROWS, 128))
     m2 = jnp.broadcast_to(jnp.sum(s2, axis=-1, keepdims=True) * (1.0 / D), (ROWS, 128))
     stats[2] = m1
     stats[3] = m2
 
     gycopies = []
-    for t in range(4):
+    for t in order_t:
         zz = (h + t) % 4
         total = gbuf[zz, :, x].astype(F32)
-        for k in range(1, 4):
-            dst = xland.at[t, k - 1]
-            remote(dst, dst, gxs_sem.at[t, k], gxr_sem.at[t, k], other).wait_recv()
-            total = total + xland[t, k - 1].astype(F32)
+        for k in range(2):
+            dst = xland.at[t, k]
+            remote(dst, dst, gxs_sem.at[t, k + 1], gxr_sem.at[t, k + 1], other).wait_recv()
+            total = total + xland[t, k].astype(F32)
         ysend[t] = total.astype(BF16)
         for e in range(2):
             if t == 0 and e == 0:
@@ -377,7 +435,7 @@
     zsend[3] = tb[2]
     gzcopies = []
     for i in range(2):
-        zt = c * 8 + h + 4 * i
+        zt = c * 8 + 2 * h + i
         cp = remote(
             zsend.at[pl.ds(2 * i, 2)], zland2.at[z], gzs_sem.at[i], gzr_sem.at[z], device(zt, x, y, c)
         )
@@ -414,7 +472,7 @@
 
     @pl.when(own)
     def _():
-        second = zlow // 4
+        second = zlow % 2
         total = zsend[pl.ds(2 * second, 2)].astype(F32)
         for k in (1, 15, 2, 14, 3, 13, 4, 12, 5, 11, 6, 10, 7, 9, 8):
             dst = zland2.at[(z + k) % 16]
@@ -445,7 +503,7 @@
 
     jcopy.wait_send()
     gcopy.wait_send()
-    for cp in xcopies + list(ycopies.values()) + ccopies + qcopies + gxcopies + gycopies:
+    for cp in xcopies + ycopies + ccopies + qcopies + gxcopies + gycopies:
         cp.wait_send()
     for zt, cp in gzcopies:
 
@@ -459,19 +517,26 @@
     vmem = pl.BlockSpec(memory_space=pltpu.VMEM)
     scratch = [
         pltpu.VMEM((ROWS, D), BF16),
+        pltpu.VMEM((24, 192), BF16),
+        pltpu.VMEM((1, 4 * ROWS), jnp.int32),
+        pltpu.VMEM((40, 128), BF16),
+        pltpu.VMEM((4, 3, 2, 48, 128), BF16),
+        pltpu.VMEM((4, 3, 2, 48, 128), BF16),
+        dma((7,)),
+        pltpu.VMEM((ROWS, D), BF16),
         pltpu.VMEM((2 * ROWS, HALF), BF16),
         pltpu.VMEM((HALF, 2 * ROWS), BF16),
         pltpu.VMEM((4, ROWS, 128), F32),
-        pltpu.VMEM((8, 2, 24, 192), BF16),
+        pltpu.VMEM((8, 2, 40, 128), BF16),
         pltpu.VMEM((2, 4, 3, 4, 2, 48, 128), BF16),
         pltpu.VMEM((2, ROWS, 192), F32),
         pltpu.VMEM((ROWS, 192), F32),
         pltpu.VMEM((4, ROWS, 128), BF16),
         pltpu.VMEM((4, 64, 128), BF16),
-        pltpu.VMEM((4, ROWS, HD), BF16),
+        pltpu.VMEM((4, HD, ROWS), BF16),
         pltpu.VMEM((2, 3, ROWS, 128), BF16),
         pltpu.VMEM((4, 3, 4, 2, 48, 128), BF16),
-        pltpu.VMEM((4, 3, 3, 2, 48, 128), BF16),
+        pltpu.VMEM((4, 2, 3, 2, 48, 128), BF16),
         pltpu.VMEM((4, 3, 2, 48, 128), BF16),
         pltpu.VMEM((8, 3, 48, 128), BF16),
         pltpu.VMEM((4, 48, 128), BF16),
@@ -496,19 +561,19 @@
     out, pg, gw = pl.pallas_call(
         kernel,
         out_shape=(
-            jax.ShapeDtypeStruct((ROWS, HD), BF16),
-            jax.ShapeDtypeStruct((ROWS, D), BF16),
-            jax.ShapeDtypeStruct((24, 192), F32),
+            pltpu.VMEM((HD, ROWS), BF16),
+            pltpu.VMEM((ROWS, D), BF16),
+            pltpu.VMEM((24, 192), F32),
         ),
-        in_specs=[vmem] * 4,
+        in_specs=[pl.BlockSpec(memory_space=pltpu.HBM)] * 4,
         out_specs=(vmem,) * 3,
         scratch_shapes=scratch,
         compiler_params=pltpu.CompilerParams(
-            collective_id=0, has_side_effects=True, vmem_limit_bytes=48 * 2**20
+            collective_id=0, has_side_effects=True, vmem_limit_bytes=56 * 2**20
         ),
         name="head",
-    )(patches[0], projection, image_ids, cotangent[0])
-    return out[None], pg[None], gw
+    )(patches[0], projection, image_ids, cotangent[0].T)
+    return out.T[None], pg[None], gw
 
 
 def solution(mesh):

time: 99.8 us -> 90.6 us (0.908)
  the two profiles are of different devices: /device:TPU:65 before, /device:TPU:49 now
where the time goes in v2:
time: 90.6 us; the launch traced here: 90.4 us
  Pallas kernels  87.4 us (96%)
  local copies, waits for them, and re-layouts  2.36 us (3%)
    pallas_call x1, Pallas kernels, per_device(): pl.pallas_call(kernel, out_shape=(pltpu.VMEM((HD, ROWS), BF16), pltpu.VME...  87.4 us
    unnamed x3, local copies, waits for them, and re-layouts  2.36 us

profile of v2, /device:TPU:49, one launch (start us, length us, event | category | flops | bytes accessed | tf_op | source)
XLA Modules:
  0.0 90.4 jit_solution(18078313688139676415)
XLA Ops:
  0.6 87.4 %head.1 = (bf16[64,128]{1,0:T(8,128)(2,1)S(1)}, bf16[128,6144]{1,0:T(8,128)(2,1)S(1)}, f32[24,192]{1,0:T(8,128)S(1)}) custom-call(bf16[128,6144]{1,0:T(8,128)(2,1)} %bitcast.10, bf16[24,192]{1,0:T(8,128)(2,1)} %w_hbm.1, s32[1,512]{1,0:T(1,128)} %ids_hbm.1, bf16[64,128]{1,0:T(8,128)(2,1)} %bitcast.11), custom_call_target="tpu_custom_call" | custom-call | tf_op jit(solution)/shard_map/head/pallas_call | solution.py:561
  88.0 0.6 copy.10
  88.6 1.1 %copy.11 = bf16[1,128,6144]{2,1,0:T(8,128)(2,1)} copy(bf16[1,128,6144]{2,1,0:T(8,128)(2,1)S(1)} %bitcast.8) | data formatting | bytes 3145728
  89.8 0.6 copy.12

commit v3 on v2

--- a/solution.py
+++ b/solution.py
@@ -70,9 +70,6 @@
     w_load = pltpu.make_async_copy(w_hbm, w_ref, in_sem.at[4])
     ids_load = pltpu.make_async_copy(ids_hbm, ids_ref, in_sem.at[5])
     cot_load = pltpu.make_async_copy(cot_hbm, cot_all.at[0], in_sem.at[6])
-    for cp in [w_load, *loads, ids_load, cot_load]:
-        cp.start()
-
     bar = pltpu.get_barrier_semaphore()
 
     def signal(dev):
@@ -103,6 +100,9 @@
     expected = (
         15 + jnp.where(home, 0, 1) + jnp.where(own, 8, 2) + 1 + 3 + 7
     )
+
+    for cp in [w_load, *loads, ids_load, cot_load]:
+        cp.start()
 
     def norm_body(i, carry):
         rows = pl.ds(pl.multiple_of(i * 16, 16), 16)
@@ -131,7 +131,7 @@
     pl.semaphore_wait(bar, expected)
 
     zcopies = []
-    for k in (1, 15, 2, 14, 3, 13, 4, 12, 5, 11, 6, 10, 7, 9, 8):
+    for k in (8, 1, 15, 7, 9, 2, 14, 6, 10, 3, 13, 5, 11, 4, 12):
         cp = remote(wpack, zland.at[zlow, c], zs_sem.at[k], zr_sem.at[zlow, c], device((z + k) % 16, x, y, zhalf))
         cp.start()
         zcopies.append(cp)
@@ -159,15 +159,10 @@
         cp = remote(cot_all.at[0], cot_all.at[4 - k], qs_sem.at[2, k], qr_sem.at[2, k], device(z, x, (y + 2 * k) % 8, c))
         cp.start()
         ccopies.append(cp)
-    nlocal.wait()
-    ncopy.wait()
-
     def tr_body(i, carry):
         col = pl.ds(pl.multiple_of(i * BLK, BLK), BLK)
         ntr[col, :] = nall[:, col].T
         return carry
-
-    lax.fori_loop(0, 8, tr_body, 0)
 
     near = []
     for zz in range(4):
@@ -212,18 +207,17 @@
         for k in range(1, 4):
             src = wbuf.at[c, zz, :, (x + 4 - k) % 4, l]
             remote(src, src, xs_sem.at[t, k], xr_sem.at[t, k], other).wait_recv()
-        piece = wbuf.at[c, zz, :, :, l]
-        cp = remote(piece, piece, ys_sem.at[t], yr_sem.at[t], device(z, x, (y + (1, 7)[t % 2]) % 8, c))
-        cp.start()
-        ycopies.append(cp)
+        for i, step in enumerate((1, 7)):
+            piece = wbuf.at[c, zz, :, pl.ds(2 * i, 2), l]
+            cp = remote(piece, piece, ys_sem.at[t, i], yr_sem.at[t, i], device(z, x, (y + step) % 8, c))
+            cp.start()
+            ycopies.append(cp)
 
     def multiply(t, accs):
         zz = order[t]
-        dst = wbuf.at[c, zz, :, :, 1 - l]
-        remote(dst, dst, ys_sem.at[t], yr_sem.at[t], other).wait_recv()
-        cp = remote(wbuf.at[c, zz], wbuf.at[c, zz], ws_sem.at[t], wr_sem.at[zz], other)
-        cp.start()
-        wcopies.append(cp)
+        for i in range(2):
+            dst = wbuf.at[c, zz, :, pl.ds(2 * i, 2), 1 - l]
+            remote(dst, dst, ys_sem.at[t, i], yr_sem.at[t, i], other).wait_recv()
         w0 = wbuf[c, zz, 0].reshape(BLK, 128)
         w1 = wbuf[c, zz, 1].reshape(BLK, 128)
         w2 = wbuf[c, zz, 2].reshape(BLK, 128)
@@ -237,13 +231,19 @@
     accs = (jnp.zeros((2 * ROWS, 256), F32), jnp.zeros((2 * ROWS, 256), F32))
     along_x(0)
     along_x(1)
+    nlocal.wait()
+    ncopy.wait()
+    lax.fori_loop(0, 2, tr_body, 0)
     along_x(2)
     along_y(0)
+    lax.fori_loop(2, 4, tr_body, 0)
     along_x(3)
     along_y(1)
+    lax.fori_loop(4, 6, tr_body, 0)
     along_y(2)
     accs = multiply(0, accs)
     along_y(3)
+    lax.fori_loop(6, 8, tr_body, 0)
     for t in range(1, 4):
         accs = multiply(t, accs)
     acc_a, acc_b = accs
@@ -275,47 +275,48 @@
             )
             cp.start()
             qcopies.append(cp)
+    for zz in range(4):
+        cp = remote(wbuf.at[c, zz], wbuf.at[c, zz], ws_sem.at[zz], wr_sem.at[zz], other)
+        cp.start()
+        wcopies.append(cp)
     id_rows = [
         ids_ref[:, pl.ds(pl.multiple_of(((h + r) % 4) * ROWS, ROWS), ROWS)].astype(F32) for r in range(4)
     ]
     id_row = jnp.concatenate(id_rows, axis=1)
     id_cols = [jnp.broadcast_to(r, (128, 128)).T[:, :1] for r in id_rows]
-    for cp in ccopies + qcopies:
+    id_col = jnp.concatenate(id_cols, axis=0)
+    for cp in ccopies:
         cp.wait_recv()
-
-    qs, ks, vs, cots = [], [], [], []
+    cots = [cot_all[r].astype(F32).T for r in range(4)]
+    for cp in qcopies:
+        cp.wait_recv()
+
+    qs, ks, vs = [], [], []
     for r in range(4):
         both = qk_all[r].astype(F32)
         qs.append(both[:, :HD].astype(BF16))
         ks.append(both[:, HD:].astype(BF16))
         packed = v_all[r].astype(F32)
         vs.append(jnp.concatenate([packed[:, :HD], packed[:, HD:]], axis=0).astype(BF16))
-        cots.append(cot_all[r].astype(F32).T)
     k_whole = jnp.concatenate(ks, axis=0)
     v_whole = jnp.concatenate(vs, axis=0)
     factor = 1.0 / math.sqrt(HD)
-    key_grad = jnp.zeros((ROWS, HD), F32)
-    value_grad = jnp.zeros((ROWS, HD), F32)
-    query_grad = None
-    for r in range(4):
-        scores = dot_nt(qs[r], k_whole) * factor
-        expo = jnp.where(id_cols[r] == id_row, jnp.exp(scores), 0.0)
-        denom = jnp.sum(expo, axis=-1, keepdims=True)
-        probs = expo.astype(BF16)
-        attended = dot(probs, v_whole) / denom
-        scaled = (cots[r] / denom).astype(BF16)
-        correction = jnp.sum(cots[r] * attended, axis=-1, keepdims=True) / denom
-        if r == 0:
-            out_ref[...] = attended.T.astype(BF16)
-            pgrad = dot_nt(scaled, v_whole)
-            sgrad = (probs.astype(F32) * (pgrad - correction)).astype(BF16)
-            query_grad = dot(sgrad, k_whole) * factor
-            sgrad = sgrad[:, :ROWS]
-        else:
-            pgrad = dot_nt(scaled, vs[0])
-            sgrad = (probs[:, :ROWS].astype(F32) * (pgrad - correction)).astype(BF16)
-        key_grad += dot_tn(sgrad, qs[r])
-        value_grad += dot_tn(probs[:, :ROWS], scaled)
+    q_whole = jnp.concatenate(qs, axis=0)
+    cot_whole = jnp.concatenate(cots, axis=0)
+    expo = jnp.where(id_col == id_row, jnp.exp(dot_nt(q_whole, k_whole) * factor), 0.0)
+    denom = jnp.sum(expo, axis=-1, keepdims=True)
+    probs = expo.astype(BF16)
+    attended = dot(probs, v_whole) / denom
+    scaled = (cot_whole / denom).astype(BF16)
+    correction = jnp.sum(cot_whole * attended, axis=-1, keepdims=True) / denom
+    out_ref[...] = attended[:ROWS].T.astype(BF16)
+    pgrad = dot_nt(scaled[:ROWS], v_whole)
+    sgrad = (probs[:ROWS].astype(F32) * (pgrad - correction[:ROWS])).astype(BF16)
+    query_grad = dot(sgrad, k_whole) * factor
+    pgrad = dot_nt(scaled, vs[0])
+    sgrad = (probs[:, :ROWS].astype(F32) * (pgrad - correction)).astype(BF16)
+    key_grad = dot_tn(sgrad, q_whole)
+    value_grad = dot_tn(probs[:, :ROWS], scaled)
     key_grad = key_grad * factor
 
     def norm_backward(upstream, normal, inverse):
@@ -548,7 +549,7 @@
         dma((2,)),
         dma((16,)), dma((8, 2)),
         dma((4, 4)), dma((4, 4)),
-        dma((4,)), dma((4,)),
+        dma((4, 2)), dma((4, 2)),
         dma((4,)), dma((4,)),
         dma((2,)),
         dma((3, 4)), dma((3, 4)),

time: 90.6 us -> 90.9 us (level)
  no operation moved by 1% of the time
where the time goes in v3:
time: 90.9 us; the launch traced here: 90.7 us
  Pallas kernels  87.7 us (96%)
  local copies, waits for them, and re-layouts  2.36 us (3%)
    pallas_call x1, Pallas kernels, per_device(): pl.pallas_call(kernel, out_shape=(pltpu.VMEM((HD, ROWS), BF16), pltpu.VME...  87.7 us
    unnamed x3, local copies, waits for them, and re-layouts  2.36 us

profile of v3, /device:TPU:49, one launch (start us, length us, event | category | flops | bytes accessed | tf_op | source)
XLA Modules:
  0.0 90.7 jit_solution(15862377294019295947)
XLA Ops:
  0.6 87.7 %head.1 = (bf16[64,128]{1,0:T(8,128)(2,1)S(1)}, bf16[128,6144]{1,0:T(8,128)(2,1)S(1)}, f32[24,192]{1,0:T(8,128)S(1)}) custom-call(bf16[128,6144]{1,0:T(8,128)(2,1)} %bitcast.10, bf16[24,192]{1,0:T(8,128)(2,1)} %w_hbm.1, s32[1,512]{1,0:T(1,128)} %ids_hbm.1, bf16[64,128]{1,0:T(8,128)(2,1)} %bitcast.11), custom_call_target="tpu_custom_call" | custom-call | tf_op jit(solution)/shard_map/head/pallas_call | solution.py:562
  88.3 0.6 copy.10
  88.9 1.1 %copy.11 = bf16[1,128,6144]{2,1,0:T(8,128)(2,1)} copy(bf16[1,128,6144]{2,1,0:T(8,128)(2,1)S(1)} %bitcast.8) | data formatting | bytes 3145728
  90.1 0.6 copy.12
